TPU v7x, 128 devices: a whole 4x4x4 slice. The times are simulated.
128 devices in a mesh: row: 8 (over z, core), col: 16 (over y, x).
Axes of the slice: x: 4, y: 4, z: 4, core: 2. Of those that a mesh axis runs over, the one named last changes fastest.
Arguments:
- covariance: float32 [4, 8, 2, 16, 512, 512], P(None, 'row', None, 'col'), may hold values from 0 to 9.5, as said below
- migration: int32 [8, 16, 16], replicated, may hold values from -1 to 15, as said below
Outputs:
- factor: float32 [4, 8, 2, 16, 512, 512], P(None, 'row', None, 'col')
- offloaded: float32 [8, 16, 16, 512, 256], P('row', 'col')
Inputs may be any that keep to these rules, and one draw needn't show every extreme that they name: covariance is symmetric and positive definite, with smallest eigenvalue 0.5 or more. An entry t >= 0 of migration[r, s, d] names half t % 2 of the local tile t // 2 of device (r, s), and that tile A[i, j] has i >= j > 1; each half-tile is named at most once; migration[r, s, s] = -1.
All inputs are finite; a program needn't handle non-finite values.
Results may differ from a plain program's by a relative error of at most 0.0003.
Values sent between devices are 32-bit elements; how exact they have to be, the bound alone decides.
A program may use at most 192 MiB of HBM per device.

v0:
```python
import jax
import jax.numpy as jnp
from jax import lax
from jax.sharding import PartitionSpec as P


def spread(block, axis, owner):
    block = jnp.where(lax.axis_index(axis) == owner, block, jnp.zeros_like(block))
    return lax.psum(block, axis)


def solve_panel(lower, panel):
    count = panel.shape[0]
    block = panel.shape[1]
    wide = panel.transpose(2, 0, 1).reshape(block, count * block)
    solved = lax.linalg.triangular_solve(lower, wide, left_side=True, lower=True)
    return solved.reshape(block, count, block).transpose(1, 2, 0)


def outer_product(left, right):
    return lax.dot_general(
        left,
        right,
        (((1,), (1,)), ((), ())),
        precision=lax.Precision.HIGHEST,
        preferred_element_type=jnp.float32,
    )


def no_product(left, right):
    return jnp.zeros((left.shape[0], right.shape[0]), jnp.float32)


def subtract(tile, left, right):
    return tile - outer_product(left, right)


def keep(tile, left, right):
    return tile


def factor_tile(tile):
    return jnp.linalg.cholesky(tile)


def empty_tile(tile):
    return jnp.zeros_like(tile)


def per_device(covariance, migration):
    rows = lax.axis_size("row")
    cols = lax.axis_size("col")
    row_index = lax.axis_index("row")
    col_index = lax.axis_index("col")
    tiles = covariance[:, 0, :, 0]
    tile_rows = tiles.shape[0]
    tile_cols = tiles.shape[1]
    block = tiles.shape[-1]
    half_cols = block // 2
    global_rows = jnp.arange(tile_rows, dtype=jnp.int32) * rows + row_index
    global_cols = jnp.arange(tile_cols, dtype=jnp.int32) * cols + col_index
    tile_list = [[tiles[l, m] for m in range(tile_cols)] for l in range(tile_rows)]

    def masked(solved, lower, step):
        place = global_rows[:, None, None]
        return jnp.where(
            place > step, solved, jnp.where(place == step, lower[None], jnp.zeros_like(solved))
        )

    def panel_step(step):
        root_row = step % rows
        root_col = step % cols
        local_row = step // rows
        local_col = step // cols
        on_column = col_index == root_col
        is_root = (row_index == root_row) & on_column
        factored = lax.cond(is_root, factor_tile, empty_tile, tile_list[local_row][local_col])
        column_tiles = jnp.stack([tile_list[l][local_col] for l in range(tile_rows)])
        lower = spread(factored, "row", root_row)

        def solve_here(stack):
            return masked(solve_panel(lower, stack), lower, step)

        def skip_here(stack):
            return jnp.zeros_like(stack)

        outgoing = lax.cond(on_column, solve_here, skip_here, column_tiles)
        received = spread(outgoing, "col", root_col)
        grouped = received.reshape(tile_cols, cols // rows, block, block)
        picked = lax.dynamic_index_in_dim(grouped, col_index // rows, axis=1, keepdims=False)
        partners = spread(picked, "row", col_index % rows)
        return (received, partners)

    def place_column(step, panel):
        for l in range(tile_rows):
            for m in range(tile_cols):
                chosen = (global_cols[m] == step) & (global_rows[l] >= step)
                tile_list[l][m] = jnp.where(chosen, panel[l], tile_list[l][m])

    first_panel, first_partners = panel_step(0)
    for l in range(tile_rows):
        for m in range(tile_cols):
            active = (global_rows[l] >= global_cols[m]) & (global_cols[m] > 0)
            tile_list[l][m] = lax.cond(
                active, subtract, keep, tile_list[l][m], first_panel[l], first_partners[m]
            )
    place_column(0, first_panel)
    second_panel, second_partners = panel_step(1)
    plan_rows = lax.dynamic_index_in_dim(migration, row_index, 0, keepdims=False)
    my_plan = lax.dynamic_index_in_dim(plan_rows, col_index, 0, keepdims=False)
    chosen_out = jnp.maximum(my_plan, 0)
    live_out = my_plan >= 0
    products = []
    for l in range(tile_rows):
        for m in range(tile_cols):
            active = (global_rows[l] >= global_cols[m]) & (global_cols[m] > 1)
            product = lax.cond(
                active, outer_product, no_product, second_panel[l], second_partners[m]
            )
            tile_list[l][m] = tile_list[l][m] - product
            products.append(product)
    stacked = jnp.stack(products)
    picked = jnp.take(stacked, chosen_out // 2, axis=0)
    halves = jnp.where(
        (chosen_out % 2 == 0)[:, None, None], picked[:, :, :half_cols], picked[:, :, half_cols:]
    )
    outgoing = jnp.where(live_out[:, None, None], halves, jnp.zeros_like(halves))
    offloaded = lax.all_to_all(outgoing, "col", split_axis=0, concat_axis=0, tiled=True)
    place_column(1, second_panel)
    result_rows = []
    for l in range(tile_rows):
        result_cols = []
        for m in range(tile_cols):
            upper = global_rows[l] < global_cols[m]
            result_cols.append(jnp.where(upper, jnp.zeros_like(tile_list[l][m]), tile_list[l][m]))
        result_rows.append(jnp.stack(result_cols))
    result = jnp.stack(result_rows)
    return (result[:, None, :, None], offloaded[None, None])


def solution(mesh):
    return jax.shard_map(
        per_device,
        mesh=mesh,
        in_specs=(P(None, "row", None, "col", None, None), P()),
        out_specs=(P(None, "row", None, "col", None, None), P("row", "col", None, None, None)),
        check_vma=False,
    )
```

profile of v0, /device:TPU:97, one launch (start us, length us, event | category | flops | bytes accessed | tf_op | source)
XLA Modules:
  0.0 1068.3 jit_solution(18278794902027828453)
XLA Ops:
  7.2 8.0 slice_bitcast_fusion.24
  20.1 4.6 pad_maximum_fusion.2
  24.7 129.9 %all-reduce.8.cloned.1.call-done = f32[512,512]{1,0:T(8,128)} async-done(((f32[512,512]{1,0:T(8,128)}), f32[512,512]{1,0:T(8,128)}) %all-reduce.8.cloned.1.call-update) | async-done | bytes 1048592 | tf_op jit(solution)/shard_map/psum | solution.py:9
  154.7 90.9 %conditional.21 = (f32[4,512,512]{2,1,0:T(8,128)}) conditional(s32[]{:T(128)} %convert_element_type.109, () %tuple.163, (s32[4]{0:T(128)S(1)}, f32[4,512,512]{2,1,0:T(8,128)}, f32[512,512]{1,0:T(8,128)}) %tuple.165), branch_computations={%region_11.13_spmd, %region_12.15_spmd} | conditional | flops 4035182592 | bytes 77333792 | solution.py:87
  157.6 10.1 while.4
  167.7 40.3 %custom-call.30 = f32[4,128,128]{1,2,0:T(8,128)S(1)} custom-call(f32[4,128,128]{2,1,0:T(8,128)} %get-tuple-element.250), custom_call_target="InvertDiagBlocksLowerTriangular" | custom-call | tf_op jit(solution)/shard_map/cond/branch_1_fun/triangular_solve/custom-call.1 | solution.py:16
  219.2 5.6 fusion.18
  228.4 6.0 reshape.271
  234.4 5.6 bitcast_select_fusion
  240.0 5.2 copy.16
  245.6 4.7 broadcast_select_fusion.2
  250.4 98.9 %all-reduce.10.cloned.1.call-done = f32[4,512,512]{2,1,0:T(8,128)} async-done(((f32[4,512,512]{2,1,0:T(8,128)}), f32[4,512,512]{2,1,0:T(8,128)}) %all-reduce.10.cloned.1.call-update) | async-done | bytes 4194320 | tf_op jit(solution)/shard_map/psum | solution.py:9
  366.6 50.7 %all-reduce.12.cloned.1.call-done = f32[2,512,512]{2,1,0:T(8,128)} async-done(((f32[2,512,512]{2,1,0:T(8,128)}), f32[2,512,512]{2,1,0:T(8,128)}) %all-reduce.12.cloned.1.call-update) | async-done | bytes 2097168 | tf_op jit(solution)/shard_map/psum | solution.py:9
  433.7 154.2 %all-reduce.14.cloned.1.call-done = f32[512,512]{1,0:T(8,128)} async-done(((f32[512,512]{1,0:T(8,128)}), f32[512,512]{1,0:T(8,128)}) %all-reduce.14.cloned.1.call-update) | async-done | bytes 1048592 | tf_op jit(solution)/shard_map/psum | solution.py:9
  588.0 10.4 conditional.27
  601.0 184.4 %all-reduce.16.cloned.1.call-done = f32[4,512,512]{2,1,0:T(8,128)} async-done(((f32[4,512,512]{2,1,0:T(8,128)}), f32[4,512,512]{2,1,0:T(8,128)}) %all-reduce.16.cloned.1.call-update) | async-done | bytes 4194320 | tf_op jit(solution)/shard_map/psum | solution.py:9
  800.0 53.4 %all-reduce.18.cloned.1.call-done = f32[2,512,512]{2,1,0:T(8,128)} async-done(((f32[2,512,512]{2,1,0:T(8,128)}), f32[2,512,512]{2,1,0:T(8,128)}) %all-reduce.18.cloned.1.call-update) | async-done | bytes 2097168 | tf_op jit(solution)/shard_map/psum | solution.py:9
  867.0 5.3 conditional.36
  875.6 5.3 conditional.39
  881.9 11.1 %gather_fusion = f32[16,512,512]{2,1,0:T(8,128)} fusion(f32[8,512,512]{2,1,0:T(8,128)} %constant_dynamic-update-slice_fusion.8, s32[1024]{0:T(1024)S(1)} %pad_clamp_fusion), kind=kCustom, calls=%fused_computation | custom fusion | bytes 33554496 | tf_op jit(solution)/shard_map/jit(_take)/gather | solution.py:123
  893.0 7.1 broadcast_select_fusion
  904.7 20.7 %all-to-all-start = ((f32[16,512,256]{2,1,0:T(8,128)}), f32[16,512,256]{2,1,0:T(8,128)}, u32[]{:S(2)}, u32[]{:S(2)}) async-start(f32[16,512,256]{2,1,0:T(8,128)} %fusion.70), calls=%async_computation | async-start | bytes 16777216 | tf_op jit(solution)/shard_map/all_to_all | solution.py:128
  969.4 84.3 %all-to-all-done = f32[16,512,256]{2,1,0:T(8,128)} async-done(((f32[16,512,256]{2,1,0:T(8,128)}), f32[16,512,256]{2,1,0:T(8,128)}, u32[]{:S(2)}, u32[]{:S(2)}) %all-to-all-start) | async-done | bytes 8388640 | tf_op jit(solution)/shard_map/all_to_all | solution.py:128
  1053.7 7.5 copy.122
  (143 shorter events, 150.2 us)
Async XLA Ops:
  7.2 147.5 %all-reduce.8.cloned.1.call-start = ((), (), s32[]{:S(2)}) async-start(), calls=%async_computation.1 | async-start | bytes 2097152 | tf_op jit(solution)/shard_map/psum | solution.py:9
  20.1 329.2 %all-reduce.10.cloned.1.call-start = ((), (), s32[]{:S(2)}) async-start(), calls=%async_computation.2 | async-start | bytes 8388608 | tf_op jit(solution)/shard_map/psum | solution.py:9
  208.0 6.6 copy-start.4
  250.3 167.0 %all-reduce.12.cloned.1.call-start = ((), (), s32[]{:S(2)}) async-start(), calls=%async_computation.3 | async-start | bytes 4194304 | tf_op jit(solution)/shard_map/psum | solution.py:9
  352.5 235.5 %all-reduce.14.cloned.1.call-start = ((), (), s32[]{:S(2)}) async-start(), calls=%async_computation.4 | async-start | bytes 2097152 | tf_op jit(solution)/shard_map/psum | solution.py:9
  423.6 5.7 copy-start.2
  429.3 356.1 %all-reduce.16.cloned.1.call-start = ((), (), s32[]{:S(2)}) async-start(), calls=%async_computation.5 | async-start | bytes 8388608 | tf_op jit(solution)/shard_map/psum | solution.py:9
  600.9 252.5 %all-reduce.18.cloned.1.call-start = ((), (), s32[]{:S(2)}) async-start(), calls=%async_computation.6 | async-start | bytes 4194304 | tf_op jit(solution)/shard_map/psum | solution.py:9
  853.4 1.9 copy-start.16
  904.7 35.7 %copy-start.13 = (f32[512,512]{1,0:T(8,128)S(1)}, f32[512,512]{1,0:T(8,128)}, u32[]{:S(2)}) copy-start(f32[512,512]{1,0:T(8,128)} %get-tuple-element.312) | copy-start | bytes 3145732
  904.7 149.1 %all-to-all-start = ((f32[16,512,256]{2,1,0:T(8,128)}), f32[16,512,256]{2,1,0:T(8,128)}, u32[]{:S(2)}, u32[]{:S(2)}) async-start(f32[16,512,256]{2,1,0:T(8,128)} %fusion.70), calls=%async_computation | async-start | bytes 16777216 | tf_op jit(solution)/shard_map/all_to_all | solution.py:128
  925.4 15.0 %copy-start.10 = (f32[512,512]{1,0:T(8,128)S(1)}, f32[512,512]{1,0:T(8,128)}, u32[]{:S(2)}) copy-start(f32[512,512]{1,0:T(8,128)} %get-tuple-element.317) | copy-start | bytes 3145732
  940.4 3.8 copy-start.14
  944.2 1.0 copy-start.11
  945.1 4.7 copy-start.6
  945.1 4.7 copy-start.8
  949.8 4.1 copy-start
  949.9 5.3 copy-start.1
  949.9 5.5 copy-start.7
  949.9 5.8 copy-start.9
  955.7 2.7 copy-start.3
  955.7 2.7 copy-start.17
  960.9 1.2 copy-start.12
  960.9 1.5 copy-start.15
Sparse Core Ops, SparseCore 0:
  20.2 134.4 all-reduce.7
  250.5 98.8 all-reduce.9
  352.6 64.7 all-reduce.11
  429.4 158.5 all-reduce.13
  601.1 184.2 all-reduce.15
  788.7 64.7 all-reduce.17
where the time goes:
time: 1080 us; the launch traced here: 1070 us
  waiting for transfers between devices  756 us (70%)
  other arithmetic  108 us (10%)
  local copies, waits for them, and re-layouts  88.9 us (8%)
  between operations  44.5 us (4%)
  matrix products  34.2 us (3%)
  starting transfers between devices  20.9 us (2%)
  loops' own time  15.7 us (1%)
    psum x6, waiting for transfers between devices, spread(): return lax.psum(block, axis)  672 us
    all_to_all x1, waiting for transfers between devices, per_device(): lax.all_to_all(outgoing, 'col', split_axis=0, concat_axis=0, tiled=True)  84.3 us
    another operation x5, other arithmetic, solve_panel(): lax.linalg.triangular_solve(lower, wide, left_side=True, lower=True)  44.2 us
  transfers between devices with their start and end apart: 7, of which 7 were waited for; matrix products, arithmetic and copies ran while one was open for 4% of the time, Pallas kernels for 0%

commit v1 on v0

--- a/solution.py
+++ b/solution.py
@@ -6,7 +6,7 @@
 
 def spread(block, axis, owner):
     block = jnp.where(lax.axis_index(axis) == owner, block, jnp.zeros_like(block))
-    return lax.psum(block, axis)
+    return jnp.sum(lax.all_gather(block, axis), axis=0)
 
 
 def solve_panel(lower, panel):

time: 1080 us -> 1750 us (1.62)
  waiting for transfers between devices: 756 us -> 1250 us
  local copies, waits for them, and re-layouts: 88.9 us -> 175 us
  other arithmetic: 108 us -> 169 us
    all_gather x0 -> x6, waiting for transfers between devices: none -> 1200 us  [spread(): return jnp.sum(lax.all_gather(block, axis), axis=0)]
    psum x6 -> x0, waiting for transfers between devices: 672 us -> none  [spread(): return lax.psum(block, axis)]
    reduce_sum x0 -> x5, other arithmetic: none -> 68.6 us  [spread(): return jnp.sum(lax.all_gather(block, axis), axis=0)]
    cond x4 -> x14, local copies, waits for them, and re-layouts: 2.46 us -> 40.5 us  [the longest x8 17.7 us: per_device(): lax.cond(active, subtract, keep, tile_list[l][m], first_panel[l], first_p...]
    unnamed x40 -> x53, local copies, waits for them, and re-layouts: 18.7 us -> 54.9 us
    all_to_all x1, waiting for transfers between devices: 84.3 us -> 56.6 us  [per_device(): lax.all_to_all(outgoing, 'col', split_axis=0, concat_axis=0, tiled=True)]
  transfers between devices with their start and end apart: 7 -> 7, of which waited for: 7 -> 7; matrix products, arithmetic and copies ran while one was open for 4% -> 5% of each run, Pallas kernels for 0% -> 0%
where the time goes in v1:
time: 1750 us; the launch traced here: 1740 us
  waiting for transfers between devices  1250 us (71%)
  local copies, waits for them, and re-layouts  175 us (10%)
  other arithmetic  169 us (10%)
  between operations  46.9 us (3%)
  matrix products  36 us (2%)
  starting transfers between devices  28.7 us (2%)
  loops' own time  25.2 us (1%)
    all_gather x6, waiting for transfers between devices, spread(): return jnp.sum(lax.all_gather(block, axis), axis=0)  1200 us
    reduce_sum x5, other arithmetic, spread(): return jnp.sum(lax.all_gather(block, axis), axis=0)  68.6 us
    all_to_all x1, waiting for transfers between devices, per_device(): lax.all_to_all(outgoing, 'col', split_axis=0, concat_axis=0, tiled=True)  56.6 us
    unnamed x53, local copies, waits for them, and re-layouts  54.9 us
    another operation x5, other arithmetic, solve_panel(): lax.linalg.triangular_solve(lower, wide, left_side=True, lower=True)  42.9 us
  transfers between devices with their start and end apart: 7, of which 7 were waited for; matrix products, arithmetic and copies ran while one was open for 5% of the time, Pallas kernels for 0%

profile of v1, /device:TPU:97, one launch (start us, length us, event | category | flops | bytes accessed | tf_op | source)
XLA Modules:
  0.0 1735.5 jit_solution(16865494360858092107)
XLA Ops:
  7.2 7.9 slice_bitcast_fusion.21
  15.2 9.2 conditional.20
  30.2 113.5 %all-gather.13.cloned.1.call-done = f32[4096,512]{0,1:T(8,128)} async-done(((f32[512,512]{0,1:T(8,128)}), f32[4096,512]{0,1:T(8,128)}) %all-gather.13.cloned.1.call-update) | async-done | bytes 8388624 | tf_op jit(solution)/shard_map/all_gather | solution.py:9
  143.6 111.6 %conditional.21 = (f32[4,512,512]{2,1,0:T(8,128)}) conditional(s32[]{:T(128)} %convert_element_type.109, () %tuple.163, (s32[4]{0:T(128)S(1)}, f32[4,512,512]{2,1,0:T(8,128)}, f32[4096,512]{0,1:T(8,128)}, f32[]{:T(128)}) %tuple.165), branch_computations={%region_11.13_spmd, %region_12.15_spmd} | conditional | flops 4037017600 | bytes 120324400 | solution.py:87
  155.3 11.5 copy.208
  171.7 11.5 while.4
  183.2 39.3 %custom-call.30 = f32[4,128,128]{1,2,0:T(8,128)S(1)} custom-call(f32[4,128,128]{2,1,0:T(8,128)S(1)} %get-tuple-element.250), custom_call_target="InvertDiagBlocksLowerTriangular" | custom-call | tf_op jit(solution)/shard_map/cond/branch_1_fun/triangular_solve/custom-call.1 | solution.py:16
  260.0 365.5 %all-gather.15.cloned.1.call-done = f32[64,512,512]{2,1,0:T(8,128)} async-done(((f32[4,512,512]{2,1,0:T(8,128)}), f32[64,512,512]{2,1,0:T(8,128)}) %all-gather.15.cloned.1.call-update) | async-done | bytes 67108880 | tf_op jit(solution)/shard_map/all_gather | solution.py:9
  625.5 23.1 %reduce_sum.55 = f32[4,512,512]{2,1,0:T(8,128)} reduce(f32[16,4,512,512]{3,2,1,0:T(8,128)} %bitcast.43, f32[]{:T(128)} %constant.263.clone.1), dimensions={0}, to_apply=%region_13.16 | reduce | flops 15728640 | bytes 71303168 | tf_op jit(solution)/shard_map/reduce_sum | solution.py:9
  660.8 74.5 %all-gather.17.cloned.1.call-done = f32[16,1,512,512]{3,2,1,0:T(8,128)} async-done(((f32[2,1,512,512]{3,2,1,0:T(8,128)}), f32[16,1,512,512]{3,2,1,0:T(8,128)}) %all-gather.17.cloned.1.call-update) | async-done | bytes 16777232 | tf_op jit(solution)/shard_map/all_gather | solution.py:9
  735.3 9.4 bitcast_reduce_fusion.3
  782.2 110.2 %all-gather.19.cloned.1.call-done = f32[4096,512]{0,1:T(8,128)} async-done(((f32[512,512]{0,1:T(8,128)}), f32[4096,512]{0,1:T(8,128)}) %all-gather.19.cloned.1.call-update) | async-done | bytes 8388624 | tf_op jit(solution)/shard_map/all_gather | solution.py:9
  892.5 9.9 conditional.27
  904.9 471.0 %all-gather.21.cloned.1.call-done = f32[64,512,512]{2,1,0:T(8,128)} async-done(((f32[4,512,512]{2,1,0:T(8,128)}), f32[64,512,512]{2,1,0:T(8,128)}) %all-gather.21.cloned.1.call-update) | async-done | bytes 67108880 | tf_op jit(solution)/shard_map/all_gather | solution.py:9
  1376.0 23.1 %reduce_sum.58 = f32[4,512,512]{2,1,0:T(8,128)} reduce(f32[16,4,512,512]{3,2,1,0:T(8,128)} %bitcast.64, f32[]{:T(128)} %constant.263.clone.1), dimensions={0}, to_apply=%region_28.31 | reduce | flops 15728640 | bytes 71303168 | tf_op jit(solution)/shard_map/reduce_sum | solution.py:9
  1422.3 63.5 %all-gather.23.cloned.1.call-done = f32[16,1,512,512]{3,2,1,0:T(8,128)} async-done(((f32[2,1,512,512]{3,2,1,0:T(8,128)}), f32[16,1,512,512]{3,2,1,0:T(8,128)}) %all-gather.23.cloned.1.call-update) | async-done | bytes 16777232 | tf_op jit(solution)/shard_map/all_gather | solution.py:9
  1485.7 9.4 bitcast_reduce_fusion.2
  1519.9 8.2 conditional.36
  1534.3 8.5 conditional.39
  1545.0 11.1 gather_fusion
  1567.6 28.4 %all-to-all-start = ((f32[16,512,256]{2,1,0:T(8,128)}), f32[16,512,256]{2,1,0:T(8,128)}, u32[]{:S(2)}, u32[]{:S(2)}) async-start(f32[16,512,256]{2,1,0:T(8,128)} %fusion.70), calls=%async_computation | async-start | bytes 16777216 | tf_op jit(solution)/shard_map/all_to_all | solution.py:128
  1626.0 8.7 conditional.38
  1654.5 9.9 copy.120
  1664.4 56.6 %all-to-all-done = f32[16,512,256]{2,1,0:T(8,128)} async-done(((f32[16,512,256]{2,1,0:T(8,128)}), f32[16,512,256]{2,1,0:T(8,128)}, u32[]{:S(2)}, u32[]{:S(2)}) %all-to-all-start) | async-done | bytes 8388640 | tf_op jit(solution)/shard_map/all_to_all | solution.py:128
  (176 shorter events, 276.9 us)
Async XLA Ops:
  7.2 136.5 %all-gather.13.cloned.1.call-start = ((), (), s32[]{:S(2)}) async-start(), calls=%async_computation.1 | async-start | bytes 9437184 | tf_op jit(solution)/shard_map/all_gather | solution.py:9
  25.5 600.0 %all-gather.15.cloned.1.call-start = ((), (), s32[]{:S(2)}) async-start(), calls=%async_computation.2 | async-start | bytes 71303168 | tf_op jit(solution)/shard_map/all_gather | solution.py:9
  222.6 5.8 copy-start.11
  260.0 475.3 %all-gather.17.cloned.1.call-start = ((), (), s32[]{:S(2)}) async-start(), calls=%async_computation.3 | async-start | bytes 18874368 | tf_op jit(solution)/shard_map/all_gather | solution.py:9
  651.8 240.6 %all-gather.19.cloned.1.call-start = ((), (), s32[]{:S(2)}) async-start(), calls=%async_computation.4 | async-start | bytes 9437184 | tf_op jit(solution)/shard_map/all_gather | solution.py:9
  748.3 31.5 %copy-start = (f32[512,512]{0,1:T(8,128)}, f32[512,512]{0,1:T(8,128)S(1)}, u32[]{:S(2)}) copy-start(f32[512,512]{0,1:T(8,128)S(1)} %broadcast_select_fusion.8) | copy-start | bytes 3145732
  756.2 619.7 %all-gather.21.cloned.1.call-start = ((), (), s32[]{:S(2)}) async-start(), calls=%async_computation.5 | async-start | bytes 71303168 | tf_op jit(solution)/shard_map/all_gather | solution.py:9
  769.0 8.5 copy-start.2
  904.9 580.8 %all-gather.23.cloned.1.call-start = ((), (), s32[]{:S(2)}) async-start(), calls=%async_computation.6 | async-start | bytes 18874368 | tf_op jit(solution)/shard_map/all_gather | solution.py:9
  1495.1 1.9 copy-start.7
  1531.6 2.7 copy-start.15
  1567.6 44.5 %copy-start.6 = (f32[512,512]{1,0:T(8,128)S(1)}, f32[512,512]{1,0:T(8,128)}, u32[]{:S(2)}) copy-start(f32[512,512]{1,0:T(8,128)} %get-tuple-element.454) | copy-start | bytes 3145732
  1567.6 153.4 %all-to-all-start = ((f32[16,512,256]{2,1,0:T(8,128)}), f32[16,512,256]{2,1,0:T(8,128)}, u32[]{:S(2)}, u32[]{:S(2)}) async-start(f32[16,512,256]{2,1,0:T(8,128)} %fusion.70), calls=%async_computation | async-start | bytes 16777216 | tf_op jit(solution)/shard_map/all_to_all | solution.py:128
  1612.1 2.7 copy-start.4
  1623.3 2.6 copy-start.3
  1637.6 1.2 copy-start.5
  1637.7 1.5 copy-start.10
  1637.7 1.8 copy-start.14
  1637.7 2.1 copy-start.19
  1642.1 1.5 copy-start.13
  1642.2 1.8 copy-start.18
  1646.3 1.2 copy-start.1
  1646.3 1.5 copy-start.8
  1646.3 1.8 copy-start.16
  (2 other events, 2.2 us)
Sparse Core Ops, SparseCore 0:
  25.6 117.9 all-gather.12
  260.1 365.3 all-gather.14
  651.9 83.3 all-gather.16
  756.4 136.0 all-gather.18
  905.0 470.8 all-gather.20
  1402.4 83.3 all-gather.22
